TPU v7x, 128 devices: a whole 4x4x4 slice. The times are simulated.
128 devices in a mesh: pole: 4 (over y_lo, core), dom: 32 (over z, x, y_hi).
Axes of the slice: x: 4, y: 4 (y_hi: 2, y_lo: 2; y = y_hi * 2 + y_lo), z: 4, core: 2. Of those that a mesh axis runs over, the one named last changes fastest.
Arguments:
- initial_block: bfloat16 [32, 8, 512, 256], P('dom'), may hold values from -24 to 24
- coupling: bfloat16 [32, 8, 512, 512], P('dom'), may hold values from -0.125 to 0.125
- pivots: bfloat16 [4, 32, 8, 2, 512, 512], P('pole', 'dom'), may hold values from -0.125 to 0.125
- interface: bfloat16 [4, 32, 3, 2, 512, 512], P('pole', 'dom'), may hold values from -0.1875 to 0.1875
- pole_values: float32 [4, 4], P('pole'), may hold values from 0.5 to 1.5
Outputs:
- filtered_basis: float32 [32, 8, 512, 256], P('dom', 'pole')
- rayleigh: float32 [256, 256], replicated
All inputs are finite; a program needn't handle non-finite values.
Results may differ from a plain program's by a relative error of at most 0.008.
Values sent between devices are 32-bit elements; how exact they have to be, the bound alone decides.
A program may use at most 192 MiB of HBM per device.

v0:
```python
import jax
import jax.numpy as jnp
from jax import lax
from jax.sharding import PartitionSpec as P

B = 512
M = 256


def shifted(x, axis, by):
    length = lax.axis_size(axis)
    pairs = [(i, i + by) for i in range(length) if 0 <= i + by < length]
    return lax.ppermute(x, axis, pairs)


def lower_solve(factor, right_side):
    return lax.linalg.triangular_solve(factor, right_side, left_side=True, lower=True)


def complex_product(matrix, vectors):
    block_order = matrix.shape[1]
    half_width = vectors.shape[1] // 2
    stacked = matrix.reshape(2 * block_order, block_order)
    stacked_out = jnp.dot(stacked, vectors.astype(jnp.bfloat16), preferred_element_type=jnp.float32)
    real_part = stacked_out[:block_order, :half_width] - stacked_out[block_order:, half_width:]
    imag_part = stacked_out[:block_order, half_width:] + stacked_out[block_order:, :half_width]
    return jnp.concatenate([real_part, imag_part], axis=1)


def real_product(matrix, vectors):
    return jnp.dot(matrix, vectors.astype(jnp.bfloat16), preferred_element_type=jnp.float32)


def transposed_product(matrix, vectors):
    return lax.dot_general(
        matrix,
        vectors.astype(jnp.bfloat16),
        (((0,), (0,)), ((), ())),
        preferred_element_type=jnp.float32,
    )


def inner_products(left, right_side):
    return lax.dot_general(
        left,
        right_side,
        (((0,), (0,)), ((), ())),
        precision=lax.Precision.HIGHEST,
        preferred_element_type=jnp.float32,
    )


def partition_solve(inverse, coupled, source):
    previous = jnp.roll(coupled, 1, axis=0)
    initial = jnp.zeros(source.shape[1:], jnp.float32)

    def forward_step(carried, members):
        block_inverse, given, couple_prev = members
        result = complex_product(block_inverse, given + transposed_product(couple_prev, carried))
        return (result, result)

    unused, forward = lax.scan(forward_step, initial, (inverse, source, previous))

    def backward_step(carried, members):
        block_inverse, partial_value, couple_next = members
        result = partial_value + complex_product(block_inverse, real_product(couple_next, carried))
        return (result, result)

    unused, backward = lax.scan(backward_step, initial, (inverse, forward, coupled), reverse=True)
    return backward


def on_device(initial_block, coupling, pivots, interface, pole_values):
    blocks = coupling.shape[1]
    coupled = coupling[0]
    inverse = pivots[0, 0]
    factors = interface[0, 0]
    real_start = initial_block[0].astype(jnp.float32)
    source = jnp.concatenate([real_start, jnp.zeros_like(real_start)], axis=-1)
    first = partition_solve(inverse, coupled, source)
    bottom = first[blocks - 1]
    top = first[0]
    top_next = shifted(top, "dom", -1)
    below = complex_product(factors[0], bottom) - complex_product(factors[1], top_next)
    topmost = lax.axis_index("dom") == lax.axis_size("dom") - 1
    above = jnp.where(
        topmost, jnp.zeros_like(top_next), top_next - complex_product(factors[2], below)
    )
    link = coupled[blocks - 1]
    lifted = transposed_product(link, below)
    arriving = shifted(lifted, "dom", 1)
    update = source.at[0].add(arriving)
    update = update.at[blocks - 1].add(real_product(link, above))
    second = partition_solve(inverse, coupled, update)
    real_z = pole_values[0, 0]
    imag_z = pole_values[0, 1]
    real_w = pole_values[0, 2]
    imag_w = pole_values[0, 3]
    real_x = second[..., :M]
    imag_x = second[..., M:]
    filtered_term = real_w * real_x - imag_w * imag_x
    shifted_term = (
        (real_w * real_z - imag_w * imag_z) * real_x
        - (real_w * imag_z + imag_w * real_z) * imag_x
        - real_w * real_start
    )
    count = blocks // lax.axis_size("pole")
    owned, shifted_owned = (
        lax.psum_scatter(filtered_term[None], "pole", scatter_dimension=1, tiled=True),
        lax.psum_scatter(shifted_term[None], "pole", scatter_dimension=1, tiled=True),
    )
    own_rows = owned[0].reshape(count * B, M)
    gram_part = inner_products(own_rows, own_rows)
    projected_part = inner_products(own_rows, shifted_owned[0].reshape(count * B, M))
    gram_total, projected_total = lax.psum((gram_part, projected_part), ("pole", "dom"))
    row_total = blocks * B * lax.axis_size("dom")
    gram = gram_total / row_total
    projected = projected_total / row_total
    factor = jnp.linalg.cholesky(gram)
    filtered_basis = lower_solve(factor, own_rows.T).T.reshape(1, count, B, M)
    middle = lower_solve(factor, projected)
    rayleigh = lower_solve(factor, middle.T).T
    return (filtered_basis, rayleigh)


def solution(mesh):
    in_specs = (
        P("dom", None, None, None),
        P("dom", None, None, None),
        P("pole", "dom", None, None, None, None),
        P("pole", "dom", None, None, None, None),
        P("pole", None),
    )
    out_specs = (P("dom", "pole", None, None), P())
    return jax.shard_map(
        on_device, mesh=mesh, in_specs=in_specs, out_specs=out_specs, check_vma=False
    )
```

profile of v0, /device:TPU:1, one launch (start us, length us, event | category | flops | bytes accessed | tf_op | source)
XLA Modules:
  0.0 714.3 jit_solution(7158494593496729926)
XLA Ops:
  7.2 4.2 slice_bitcast_fusion
  12.5 2.9 copy.17
  18.0 4.2 concatenate.76
  24.6 4.3 broadcast.158.clone.2
  29.7 65.2 %while.65 = (s32[]{:T(128)}, bf16[512,512]{0,1:T(8,128)(2,1)}, f32[8,512,512]{1,2,0:T(8,128)}, bf16[8,2,512,512]{3,2,1,0:T(8,128)(2,1)}, f32[8,512,512]{1,2,0:T(8,128)}, /*index=5*/bf16[8,512,512]{2,1,0:T(8,128)(2,1)}, s32[]{:T(128)}) while((s32[]{:T(128)}, bf16[512,512]{0,1:T(8,128)(2,1)}, f32[8,512,512]{1,2,0:T(8,128)}, ...), condition=%wide.region_1.2_spmd, body=%wide.region_0.1_spmd.sunk | while | flops 806617088 | bytes 17302612 | solution.py:62
  33.6 2.7 fusion.131
  41.8 2.7 fusion.131
  49.9 2.7 fusion.131
  58.1 2.7 fusion.131
  66.3 2.7 fusion.131
  90.7 2.7 fusion.131
  95.0 4.3 broadcast.158.clone.1
  99.3 67.7 %while.68 = (s32[]{:T(128)}, bf16[512,512]{0,1:T(8,128)(2,1)}, f32[8,512,512]{1,2,0:T(8,128)}, f32[8,512,512]{1,2,0:T(8,128)}, bf16[8,2,512,512]{3,2,1,0:T(8,128...) while((s32[]{:T(128)}, bf16[512,512]{0,1:T(8,128)(2,1)}, ...), condition=%wide.region_3.4_spmd.clone, body=%wide.region_2.3_spmd.clone.sunk | while | flops 807403520 | bytes 15204483 | solution.py:69
  173.9 22.7 %collective-permute-done = f32[512,512]{0,1:T(8,128)S(1)} collective-permute-done((f32[512,512]{0,1:T(8,128)S(1)}, f32[512,512]{0,1:T(8,128)S(1)}, u32[]{:S(2)}, u32[]{:S(2)}) %collective-permute-start) | collective-permute-done | bytes 1048608 | tf_op jit(solution)/shard_map/ppermute | solution.py:13
  200.3 6.9 collective-permute-start.1
  213.6 13.6 %collective-permute-done.1 = f32[512,512]{0,1:T(8,128)} collective-permute-done((f32[512,512]{0,1:T(8,128)}, f32[512,512]{0,1:T(8,128)}, u32[]{:S(2)}, u32[]{:S(2)}) %collective-permute-start.1) | collective-permute-done | bytes 1048608 | tf_op jit(solution)/shard_map/ppermute | solution.py:13
  229.5 2.9 fusion.52
  232.4 4.3 broadcast.158.clone
  237.6 65.4 %while.66 = (s32[]{:T(128)}, bf16[512,512]{0,1:T(8,128)(2,1)}, f32[8,512,512]{1,2,0:T(8,128)}, bf16[8,2,512,512]{3,2,1,0:T(8,128)(2,1)}, f32[8,512,512]{1,2,0:T(8,128)}, /*index=5*/bf16[8,512,512]{2,1,0:T(8,128)(2,1)}, s32[]{:T(128)}) while((s32[]{:T(128)}, bf16[512,512]{0,1:T(8,128)(2,1)}, f32[8,512,512]{1,2,0:T(8,128)}, ...), condition=%wide.region_5.6_spmd, body=%wide.region_4.5_spmd.sunk | while | flops 806617088 | bytes 17302612 | solution.py:62
  303.0 4.3 broadcast.158
  307.4 67.7 %while.69 = (s32[]{:T(128)}, bf16[512,512]{0,1:T(8,128)(2,1)}, f32[8,512,512]{1,2,0:T(8,128)}, f32[8,512,512]{1,2,0:T(8,128)}, bf16[8,2,512,512]{3,2,1,0:T(8,128...) while((s32[]{:T(128)}, bf16[512,512]{0,1:T(8,128)(2,1)}, ...), condition=%wide.region_7.8_spmd.clone, body=%wide.region_6.7_spmd.clone.sunk | while | flops 807403520 | bytes 15204483 | solution.py:69
  375.0 9.9 %subtract_bitcast_fusion = (f32[1,8,512,256]{2,3,1,0:T(8,128)}, f32[1,8,512,256]{2,3,1,0:T(8,128)}) fusion(f32[8,512,512]{1,2,0:T(8,128)} %get-tuple-element.338, f32[]{:T(128)S(6)} %add.169, f32[]{:T(128)S(6)} %sub.71, f32[]{:T(128)} %bitcast.8, bf16[1,8,512,256]{2,3,1,0:T(8,128)(2,1)} %copy-done.2, f32[]{:T(128)} %bitcast.27), kind=kLoop, calls=%fused_computation.61 | loop fusion | flops 9437184 | bytes 18874384 | tf_op jit(solution)/shard_map/broadcast_in_dim | solution.py:110
  386.0 51.4 %reduce-scatter.3.cloned.1.call-done = f32[1,2,512,256]{2,3,1,0:T(8,128)} async-done(((f32[1,8,512,256]{2,3,1,0:T(8,128)}), f32[1,2,512,256]{2,3,1,0:T(8,128)}) %reduce-scatter.3.cloned.1.call-update) | async-done | bytes 1048592 | tf_op jit(solution)/shard_map/reduce_scatter | solution.py:109
  437.4 3.4 convolution_bitcast_fusion.6
  440.8 45.5 %reduce-scatter.5.cloned.1.call-done = f32[1,2,512,256]{2,3,1,0:T(8,128)} async-done(((f32[1,8,512,256]{2,3,1,0:T(8,128)}), f32[1,2,512,256]{2,3,1,0:T(8,128)}) %reduce-scatter.5.cloned.1.call-update) | async-done | bytes 1048592 | tf_op jit(solution)/shard_map/reduce_scatter | solution.py:110
  486.3 3.3 convolution_bitcast_fusion.5
  490.0 148.1 %all-reduce.5.cloned.1.call-done = (f32[256,256]{0,1:T(8,128)}, f32[256,256]{0,1:T(8,128)}) async-done(((f32[256,256]{0,1:T(8,128)}, f32[256,256]{0,1:T(8,128)}), (f32[256,256]{0,1:T(8,128)}, f32[256,256]{0,1:T(8,128)})) %all-reduce.5.cloned.1.call-update) | async-done | bytes 524304 | tf_op jit(solution)/shard_map/psum | solution.py:115
  640.3 11.7 %cholesky.50 = f32[128,128]{1,0:T(8,128)S(1)} custom-call(f32[128,128]{1,0:T(8,128)S(1)} %cholesky.118), custom_call_target="Cholesky" | custom-call | tf_op jit(solution)/shard_map/jit(cholesky)/cholesky | solution.py:119
  652.1 9.8 %custom-call.17 = f32[1,128,128]{1,2,0:T(8,128)S(1)} custom-call(f32[1,128,128]{2,1,0:T(8,128)S(1)} %get-tuple-element.519), custom_call_target="InvertDiagBlocksLowerTriangular" | custom-call | tf_op jit(solution)/shard_map/jit(cholesky)/cholesky | solution.py:119
  662.4 11.9 %cholesky.105 = f32[128,128]{1,0:T(8,128)S(1)} custom-call(f32[128,128]{1,0:T(8,128)S(1)} %convolution_subtract_fusion.3), custom_call_target="Cholesky" | custom-call | tf_op jit(solution)/shard_map/jit(cholesky)/cholesky | solution.py:119
  677.0 4.0 while.67
  681.0 19.7 %custom-call.18 = f32[2,128,128]{1,2,0:T(8,128)S(1)} custom-call(f32[2,128,128]{2,1,0:T(8,128)S(1)} %get-tuple-element.354), custom_call_target="InvertDiagBlocksLowerTriangular" | custom-call | tf_op jit(solution)/shard_map/triangular_solve | solution.py:17
  (244 shorter events, 287.6 us)
Async XLA Ops:
  7.2 430.3 %reduce-scatter.3.cloned.1.call-start = ((), (), s32[]{:S(2)}) async-start(), calls=%async_computation.2 | async-start | bytes 5242880 | tf_op jit(solution)/shard_map/reduce_scatter | solution.py:109
  15.4 6.9 copy-start.2
  15.9 2.1 copy-start
  18.0 4.2 copy-start.3
  168.3 28.2 %collective-permute-start = (f32[512,512]{0,1:T(8,128)S(1)}, f32[512,512]{0,1:T(8,128)S(1)}, u32[]{:S(2)}, u32[]{:S(2)}) collective-permute-start(f32[512,512]{0,1:T(8,128)S(1)} %slice_bitcast_fusion.1), channel_id=1, source_target_pairs={{1,0},{2,1},{3,2},{4,3},{5,4},{6,5},{7,6},{8,7},{9,8},{10,9},{11,1... | collective-permute-start | bytes 3145736 | tf_op jit(solution)/shard_map/ppermute | solution.py:13
  197.3 9.9 %copy-start.5 = (f32[1,4]{1,0:T(1,128)S(1)}, f32[1,4]{1,0:T(1,128)}, u32[]{:S(2)}) copy-start(f32[1,4]{1,0:T(1,128)} %param.23) | copy-start | bytes 52
  200.3 26.9 %collective-permute-start.1 = (f32[512,512]{0,1:T(8,128)}, f32[512,512]{0,1:T(8,128)}, u32[]{:S(2)}, u32[]{:S(2)}) collective-permute-start(f32[512,512]{0,1:T(8,128)} %convolution_bitcast_fusion.4), channel_id=1, source_target_pairs={{0,1},{1,2},{2,3},{3,4},{4,5},{5,6},{6,7},{7,8},{8,9},{9,10},{10,1... | collective-permute-start | bytes 3145736 | tf_op jit(solution)/shard_map/ppermute | solution.py:13
  212.7 14.5 %copy-start.1 = (f32[8,512,256]{1,2,0:T(8,128)S(1)}, f32[8,512,256]{1,2,0:T(8,128)}, u32[]{:S(2)}) copy-start(f32[8,512,256]{1,2,0:T(8,128)} %copy-done) | copy-start | bytes 12582916
  385.0 101.3 %reduce-scatter.5.cloned.1.call-start = ((), (), s32[]{:S(2)}) async-start(), calls=%async_computation.3 | async-start | bytes 5242880 | tf_op jit(solution)/shard_map/reduce_scatter | solution.py:110
  385.7 252.3 %all-reduce.5.cloned.1.call-start = ((), (), s32[]{:S(2)}) async-start(), calls=%async_computation.4 | async-start | bytes 1048576 | tf_op jit(solution)/shard_map/psum | solution.py:115
  437.4 52.2 %copy-start.4 = (f32[1,2,512,256]{2,3,1,0:T(8,128)S(1)}, f32[1,2,512,256]{2,3,1,0:T(8,128)}, u32[]{:S(2)}) copy-start(f32[1,2,512,256]{2,3,1,0:T(8,128)} %reduce-scatter.3.cloned.1.call-done) | copy-start | bytes 3145732
Sparse Core Ops, SparseCore 0:
  385.1 52.2 reduce-scatter.2
  439.9 46.3 reduce-scatter.4
  491.8 146.2 all-reduce.4
where the time goes:
time: 726 us; the launch traced here: 714 us
  waiting for transfers between devices  282 us (39%)
  other arithmetic  176 us (24%)
  local copies, waits for them, and re-layouts  127 us (17%)
  matrix products  99.8 us (14%)
  between operations  20.6 us (3%)
  starting transfers between devices  8.56 us (1%)
    psum x1, waiting for transfers between devices, on_device(): lax.psum((gram_part, projected_part), ('pole', 'dom'))  148 us
    dot_general x35, matrix products, complex_product(): jnp.dot(stacked, vectors.astype(jnp.bfloat16), preferred_element_type=jnp...  83.1 us
    dynamic_slice x64, local copies, waits for them, and re-layouts, partition_solve(): lax.scan(forward_step, initial, (inverse, source, previous))  82.9 us
    dynamic_update_slice x32, other arithmetic, partition_solve(): lax.scan(forward_step, initial, (inverse, source, previous))  60.9 us
    reduce_scatter x1, waiting for transfers between devices, on_device(): lax.psum_scatter(filtered_term[None], 'pole', scatter_dimension=1, tiled=...  51.4 us
    reduce_scatter x1, waiting for transfers between devices, on_device(): lax.psum_scatter(shifted_term[None], 'pole', scatter_dimension=1, tiled=T...  45.5 us
    ppermute x2, waiting for transfers between devices, shifted(): return lax.ppermute(x, axis, pairs)  36.3 us
    add x16, other arithmetic, backward_step(): partial_value + complex_product(block_inverse, real_product(couple_next,...  35.2 us
  transfers between devices with their start and end apart: 5, of which 5 were waited for; matrix products, arithmetic and copies ran while one was open for 1% of the time, Pallas kernels for 0%

commit v1 on v0

v1 whole, which is shorter than its diff:
```python
import jax
import jax.numpy as jnp
from jax import lax
from jax.experimental import pallas as pl
from jax.experimental.pallas import tpu as pltpu
from jax.sharding import PartitionSpec as P

B = 512
M = 256
H = M // 2
PB = 8
PARTS = 32
F32 = jnp.float32
BF16 = jnp.bfloat16
MESH = pl.DeviceIdType.MESH


def dot_nn(left, right):
    return jnp.dot(left, right, preferred_element_type=F32)


def dot_nt(left, right):
    return lax.dot_general(left, right, (((1,), (1,)), ((), ())), preferred_element_type=F32)


def complex_rows(rows, matrix):
    out = dot_nt(rows.astype(BF16), matrix)
    real_part = out[:H, :B] - out[H:, B:]
    imag_part = out[H:, :B] + out[:H, B:]
    return jnp.concatenate([real_part, imag_part], axis=0)


def filter_kernel(
    f_hbm, u_hbm, g_hbm, i_hbm, pole_ref, y_ref, z_ref,
    f_raw, f_rows, u_mat, g_mat, i_mat, work, first_s, lifted_d,
    t_send, t_recv, c_send, c_recv, terms, core_recv, far_recv,
    f_sem, u_sem, g_sem, i_sem, t_ss, t_rs, c_ss, c_rs, q_ss, q_rs, y_ss, y_rs,
):
    pole = lax.axis_index("pole")
    dom = lax.axis_index("dom")
    core = lax.rem(pole, 2)
    side = pole // 2
    upper = lax.rem(dom + PARTS - 1, PARTS)
    lower = lax.rem(dom + 1, PARTS)
    core_mate = (2 * side + 1 - core, dom)
    side_mate = (2 * (1 - side) + core, dom)

    loads = []
    for k in range(PB):
        loads.append(
            (
                pltpu.make_async_copy(f_hbm.at[k], f_raw.at[k], f_sem.at[k]),
                pltpu.make_async_copy(g_hbm.at[k], g_mat.at[k], g_sem.at[k]),
                pltpu.make_async_copy(u_hbm.at[k], u_mat.at[k], u_sem.at[k]),
            )
        )
        for copy in loads[-1]:
            copy.start()
    interface_load = pltpu.make_async_copy(i_hbm, i_mat, i_sem)
    interface_load.start()

    barrier = pltpu.get_barrier_semaphore()
    for mate in (core_mate, side_mate, (pole, upper), (pole, lower)):
        pl.semaphore_signal(barrier, inc=1, device_id=mate, device_id_type=MESH)

    real_z = pole_ref[0, 0]
    imag_z = pole_ref[0, 1]
    real_w = pole_ref[0, 2]
    imag_w = pole_ref[0, 3]
    real_wz = real_w * real_z - imag_w * imag_z
    imag_wz = real_w * imag_z + imag_w * real_z

    def f_half(k, half):
        return f_rows[k, half * H : (half + 1) * H, :].astype(F32)

    def wait_load(k):
        pltpu.make_async_copy(f_hbm.at[k], f_raw.at[k], f_sem.at[k]).wait()
        pltpu.make_async_copy(g_hbm.at[k], g_mat.at[k], g_sem.at[k]).wait()
        f_rows[k] = f_raw[k].T

    def wait_coupling(k):
        pltpu.make_async_copy(u_hbm.at[k], u_mat.at[k], u_sem.at[k]).wait()

    def forward_step(k, half, loading):
        if loading:
            wait_load(k)
            wait_coupling(k - 1)
        lifted = dot_nn(work[k - 1].astype(BF16), u_mat[k - 1])
        rows = jnp.concatenate([lifted[:H] + f_half(k, half), lifted[H:]], axis=0)
        return rows

    def first_solve(half):
        loading = half == 0
        if loading:
            wait_load(0)
        out = dot_nt(f_rows[0, half * H : (half + 1) * H, :], g_mat[0])
        work[0] = jnp.concatenate([out[:, :B], out[:, B:]], axis=0)

        def forward(k, carry):
            work[k] = complex_rows(forward_step(k, half, loading), g_mat[k])
            return carry

        lax.fori_loop(1, PB, forward, 0)

        def backward(i, carry):
            k = PB - 2 - i
            lifted = dot_nt(work[k + 1].astype(BF16), u_mat[k])
            work[k] = work[k] + complex_rows(lifted, g_mat[k])
            return carry

        lax.fori_loop(0, PB - 1, backward, 0)
        t_send[half] = work[0]

    def t_copy(half):
        return pltpu.make_async_remote_copy(
            src_ref=t_send.at[half], dst_ref=t_recv.at[half],
            send_sem=t_ss.at[half], recv_sem=t_rs.at[half],
            device_id=(pole, upper), device_id_type=MESH,
        )

    def c_copy(half):
        return pltpu.make_async_remote_copy(
            src_ref=c_send.at[half], dst_ref=c_recv.at[half],
            send_sem=c_ss.at[half], recv_sem=c_rs.at[half],
            device_id=(pole, lower), device_id_type=MESH,
        )

    def core_copy(half, quad):
        start = 4 * quad + 2 * (1 - core)
        return pltpu.make_async_remote_copy(
            src_ref=terms.at[half, pl.ds(start, 2)], dst_ref=core_recv.at[half, quad],
            send_sem=q_ss.at[half, quad], recv_sem=q_rs.at[half, quad],
            device_id=core_mate, device_id_type=MESH,
        )

    def far_copy(half, quad):
        return pltpu.make_async_remote_copy(
            src_ref=core_recv.at[half, quad], dst_ref=far_recv.at[half],
            send_sem=y_ss.at[half], recv_sem=y_rs.at[half],
            device_id=side_mate, device_id_type=MESH,
        )

    def interface(half):
        last = dom == PARTS - 1
        t_next = jnp.where(last, 0.0, t_recv[half])
        below = first_s[half] - complex_rows(t_next, i_mat[1])
        c_send[half] = dot_nn(below.astype(BF16), u_mat[PB - 1])
        c_copy(half).start()
        above = jnp.where(last, 0.0, t_next - complex_rows(below, i_mat[2]))
        lifted_d[half] = dot_nt(above.astype(BF16), u_mat[PB - 1])

    def emit_terms(k, half):
        real_x = work[k, :H]
        imag_x = work[k, H:]
        terms[half, k, 0] = real_w * real_x - imag_w * imag_x
        terms[half, k, 1] = (
            real_wz * real_x - imag_wz * imag_x - real_w * f_half(k, half)
        )

    def second_solve(half):
        arrived = jnp.where(dom == 0, 0.0, c_recv[half])
        rows = jnp.concatenate([arrived[:H] + f_half(0, half), arrived[H:]], axis=0)
        work[0] = complex_rows(rows, g_mat[0])

        def forward(k, carry):
            work[k] = complex_rows(forward_step(k, half, False), g_mat[k])
            return carry

        lax.fori_loop(1, PB - 1, forward, 0)
        rows = forward_step(PB - 1, half, False) + lifted_d[half]
        work[PB - 1] = complex_rows(rows, g_mat[PB - 1])
        emit_terms(PB - 1, half)

        def backward(i, carry):
            k = PB - 2 - i
            lifted = dot_nt(work[k + 1].astype(BF16), u_mat[k])
            work[k] = work[k] + complex_rows(lifted, g_mat[k])
            emit_terms(k, half)
            return carry

        lax.fori_loop(0, 3, backward, 0)
        core_copy(half, 1).start()
        lax.fori_loop(3, PB - 1, backward, 0)
        core_copy(half, 0).start()

        for quad in (1, 0):
            core_copy(half, quad).wait()
            for i in range(2):
                core_recv[half, quad, i] += terms[half, 4 * quad + 2 * core + i]

            @pl.when(side == 1 - quad)
            def _():
                far_copy(half, quad).start()

    first_solve(0)
    pl.semaphore_wait(barrier, 4)
    t_copy(0).start()
    interface_load.wait()
    wait_coupling(PB - 1)
    first_s[0] = complex_rows(work[PB - 1], i_mat[0])
    first_solve(1)
    t_copy(1).start()
    first_s[1] = complex_rows(work[PB - 1], i_mat[0])
    for half in range(2):
        t_copy(half).wait()
        interface(half)
    for half in range(2):
        c_copy(half).wait()
        second_solve(half)
    for half in range(2):
        far_copy(half, 0).wait()
        for i in range(2):
            y_ref[i, half * H : (half + 1) * H, :] = core_recv[half, side, i, 0] + far_recv[half, i, 0]
            z_ref[i, half * H : (half + 1) * H, :] = core_recv[half, side, i, 1] + far_recv[half, i, 1]


def filtered_sums(f, u, g, interface, pole_values):
    own = jax.ShapeDtypeStruct((2, M, B), F32)
    dma = pltpu.SemaphoreType.DMA
    return pl.pallas_call(
        filter_kernel,
        out_shape=(own, own),
        in_specs=[pl.BlockSpec(memory_space=pl.ANY)] * 4 + [pl.BlockSpec(memory_space=pltpu.SMEM)],
        out_specs=(pl.BlockSpec(memory_space=pltpu.VMEM), pl.BlockSpec(memory_space=pltpu.VMEM)),
        scratch_shapes=[
            pltpu.VMEM((PB, B, M), BF16),
            pltpu.VMEM((PB, M, B), BF16),
            pltpu.VMEM((PB, B, B), BF16),
            pltpu.VMEM((PB, 2 * B, B), BF16),
            pltpu.VMEM((3, 2 * B, B), BF16),
            pltpu.VMEM((PB, M, B), F32),
            pltpu.VMEM((2, M, B), F32),
            pltpu.VMEM((2, M, B), F32),
            pltpu.VMEM((2, M, B), F32),
            pltpu.VMEM((2, M, B), F32),
            pltpu.VMEM((2, M, B), F32),
            pltpu.VMEM((2, M, B), F32),
            pltpu.VMEM((2, PB, 2, H, B), F32),
            pltpu.VMEM((2, 2, 2, 2, H, B), F32),
            pltpu.VMEM((2, 2, 2, H, B), F32),
            dma((PB,)), dma((PB,)), dma((PB,)), dma,
            dma((2,)), dma((2,)), dma((2,)), dma((2,)),
            dma((2, 2)), dma((2, 2)), dma((2,)), dma((2,)),
        ],
        compiler_params=pltpu.CompilerParams(
            collective_id=0, has_side_effects=True, vmem_limit_bytes=60 * 2**20
        ),
        name="filter_sums",
    )(f, u, g, interface, pole_values)


def lower_solve(factor, right_side):
    return lax.linalg.triangular_solve(factor, right_side, left_side=True, lower=True)


def row_products(left, right):
    return jnp.einsum(
        "bvk,bwk->vw", left, right,
        precision=lax.Precision.HIGHEST, preferred_element_type=F32,
    )


def on_device(initial_block, coupling, pivots, interface, pole_values):
    y_rows, z_rows = filtered_sums(
        initial_block[0],
        coupling[0],
        pivots[0, 0].reshape(PB, 2 * B, B),
        interface[0, 0].reshape(3, 2 * B, B),
        pole_values,
    )
    gram_part = row_products(y_rows, y_rows)
    projected_part = row_products(y_rows, z_rows)
    gram_total, projected_total = lax.psum((gram_part, projected_part), ("pole", "dom"))
    row_total = PB * B * PARTS
    gram = gram_total / row_total
    projected = projected_total / row_total
    factor = jnp.linalg.cholesky(gram)
    inverse = lower_solve(factor, jnp.eye(M, dtype=F32))
    filtered_basis = jnp.einsum(
        "bvk,wv->bkw", y_rows, inverse,
        precision=lax.Precision.HIGHEST, preferred_element_type=F32,
    )[None]
    middle = jnp.dot(inverse, projected, precision=lax.Precision.HIGHEST)
    rayleigh = lax.dot_general(
        middle, inverse, (((1,), (1,)), ((), ())), precision=lax.Precision.HIGHEST
    )
    return (filtered_basis, rayleigh)


def solution(mesh):
    in_specs = (
        P("dom", None, None, None),
        P("dom", None, None, None),
        P("pole", "dom", None, None, None, None),
        P("pole", "dom", None, None, None, None),
        P("pole", None),
    )
    out_specs = (P("dom", "pole", None, None), P())
    return jax.shard_map(
        on_device, mesh=mesh, in_specs=in_specs, out_specs=out_specs, check_vma=False
    )
```

time: 726 us -> 348 us (0.48); the launches traced: 714 us -> 348 us
  waiting for transfers between devices: 282 us -> 146 us
  local copies, waits for them, and re-layouts: 127 us -> 4.19 us
  other arithmetic: 176 us -> 55.9 us
  Pallas kernels: 0 us -> 114 us
  matrix products: 99.8 us -> 12.3 us
  starting transfers between devices: 8.56 us -> 0.04 us
    pallas_call x0 -> x1, Pallas kernels: none -> 114 us  [filtered_sums(): pl.pallas_call(filter_kernel, out_shape=(own, own), in_specs=[pl.BlockSpe...]
    reduce_scatter x2 -> x0, waiting for transfers between devices: 96.9 us -> none  [the longest x1 51.4 us: on_device(): lax.psum_scatter(filtered_term[None], 'pole', scatter_dimension=1, tiled=...]
    dot_general x39 -> x5, matrix products: 95.1 us -> 10.9 us  [the longest x2 6.64 us: row_products(): jnp.einsum('bvk,bwk->vw', left, right, precision=lax.Precision.HIGHEST, p...]
    dynamic_slice x64 -> x0, local copies, waits for them, and re-layouts: 82.9 us -> none  [partition_solve(): lax.scan(forward_step, initial, (inverse, source, previous))]
    dynamic_update_slice x32 -> x0, other arithmetic: 60.9 us -> none  [partition_solve(): lax.scan(forward_step, initial, (inverse, source, previous))]
    ppermute x2 -> x0, waiting for transfers between devices: 36.3 us -> none  [shifted(): return lax.ppermute(x, axis, pairs)]
    add x16 -> x0, other arithmetic: 35.2 us -> none  [backward_step(): partial_value + complex_product(block_inverse, real_product(couple_next,...]
    another operation x12 -> x6, local copies, waits for them, and re-layouts: 22.9 us -> 3.95 us
  transfers between devices with their start and end apart: 5 -> 1, of which waited for: 5 -> 1; matrix products, arithmetic and copies ran while one was open for 1% -> 0% of each run, Pallas kernels for 0% -> 0%
where the time goes in v1:
time: 348 us
  waiting for transfers between devices  146 us (42%)
  Pallas kernels  114 us (33%)
  other arithmetic  55.9 us (16%)
  between operations  15.5 us (4%)
  matrix products  12.3 us (4%)
  local copies, waits for them, and re-layouts  4.19 us (1%)
    psum x1, waiting for transfers between devices, on_device(): lax.psum((gram_part, projected_part), ('pole', 'dom'))  146 us
    pallas_call x1, Pallas kernels, filtered_sums(): pl.pallas_call(filter_kernel, out_shape=(own, own), in_specs=[pl.BlockSpe...  114 us
    another operation x6, other arithmetic, on_device(): factor = jnp.linalg.cholesky(gram)  34.1 us
    another operation x3, other arithmetic, lower_solve(): lax.linalg.triangular_solve(factor, right_side, left_side=True, lower=True)  19.7 us
  transfers between devices with their start and end apart: 1, of which 1 were waited for; matrix products, arithmetic and copies ran while one was open for 0% of the time, Pallas kernels for 0%

profile of v1, /device:TPU:1, one launch (start us, length us, event | category | flops | bytes accessed | tf_op | source)
XLA Modules:
  0.0 347.9 jit_solution(1986166493700217634)
XLA Ops:
  7.2 0.0 all-reduce.4.cloned.1.call-start
  7.2 114.1 %filter_sums.1 = (f32[2,256,512]{2,1,0:T(8,128)}, f32[2,256,512]{2,1,0:T(8,128)}) custom-call(bf16[8,512,256]{2,1,0:T(8,128)(2,1)} %bitcast.53, bf16[8,512,512]{2,1,0:T(8,128)(2,1)} %bitcast.51, bf16[8,1024,512]{2,1,0:T(8,128)(2,1)} %bitcast.50, bf16[3,1024,512]{2,1,0:T(8,128)(2,1)} %bitcast.52, f32[1,4]{1,0:T(1,128)} %pole_ref.1), custom_call_target="tpu_custom_call" | custom-call | tf_op jit(solution)/shard_map/filter_sums/pallas_call | solution.py:220
  121.3 3.3 convolution_bitcast_fusion.2
  124.6 0.0 copy-start
  124.6 3.4 convolution_bitcast_fusion.1
  128.0 0.0 all-reduce.4.cloned.1.call-update
  128.1 145.9 %all-reduce.4.cloned.1.call-done = (f32[256,256]{0,1:T(8,128)}, f32[256,256]{0,1:T(8,128)}) async-done(((f32[256,256]{0,1:T(8,128)}, f32[256,256]{0,1:T(8,128)}), (f32[256,256]{0,1:T(8,128)}, f32[256,256]{0,1:T(8,128)})) %all-reduce.4.cloned.1.call-update) | async-done | bytes 524304 | tf_op jit(solution)/shard_map/psum | solution.py:273
  274.0 0.0 copy-start.1
  274.0 1.0 broadcast_multiply_fusion
  275.0 0.1 copy.8
  275.1 1.0 fusion.1
  276.1 11.7 %cholesky.50 = f32[128,128]{1,0:T(8,128)S(1)} custom-call(f32[128,128]{1,0:T(8,128)S(1)} %cholesky.118), custom_call_target="Cholesky" | custom-call | tf_op jit(solution)/shard_map/jit(cholesky)/cholesky | solution.py:277
  287.9 9.8 %custom-call.14 = f32[1,128,128]{1,2,0:T(8,128)S(1)} custom-call(f32[1,128,128]{2,1,0:T(8,128)S(1)} %get-tuple-element.29), custom_call_target="InvertDiagBlocksLowerTriangular" | custom-call | tf_op jit(solution)/shard_map/jit(cholesky)/cholesky | solution.py:277
  297.7 0.2 constant_dynamic-update-slice_fusion.1
  297.9 0.3 convolution_subtract_fusion.1
  298.2 11.9 %cholesky.105 = f32[128,128]{1,0:T(8,128)S(1)} custom-call(f32[128,128]{1,0:T(8,128)S(1)} %convolution_subtract_fusion.1), custom_call_target="Cholesky" | custom-call | tf_op jit(solution)/shard_map/jit(cholesky)/cholesky | solution.py:277
  310.1 0.6 compare_reduce_fusion
  312.1 0.1 triangular_solve.63
  312.2 4.0 %while.1 = (s32[]{:T(128)}, f32[256,256]{1,0:T(8,128)S(1)}, s32[2,2]{1,0:T(2,128)S(1)}, f32[2,128,128]{2,1,0:T(8,128)S(1)}, s32[]{:T(128)}) while((s32[]{:T(128)}, f32[256,256]{1,0:T(8,128)S(1)}, s32[2,2]{1,0:T(2,128)S(1)}, f32[2,128,128]{2,1,0:T(8,128)S(1)}, s32[]{:T(128)}) %tuple.27), condition=%wide.while_cond, body=%wide.while_body.sunk | while | flops 2 | bytes 131189 | solution.py:253
  312.2 0.6 fusion.29
  312.8 1.4 bitcast_dynamic-update-slice_fusion.2
  314.2 0.6 fusion.29
  314.8 1.4 bitcast_dynamic-update-slice_fusion.2
  316.2 19.7 %custom-call.15 = f32[2,128,128]{1,2,0:T(8,128)S(1)} custom-call(f32[2,128,128]{2,1,0:T(8,128)S(1)} %get-tuple-element.13), custom_call_target="InvertDiagBlocksLowerTriangular" | custom-call | tf_op jit(solution)/shard_map/triangular_solve | solution.py:253
  335.8 0.3 fusion.6
  336.1 0.3 convolution_subtract_fusion
  336.4 0.3 fusion.9
  336.7 0.0 copy-done
  336.7 2.8 convolution_bitcast_fusion
  339.5 0.0 copy-done.1
  339.5 0.4 fusion.2
  339.9 1.1 fusion.4
  (10 shorter events, 0.2 us)
Async XLA Ops:
  7.2 266.8 %all-reduce.4.cloned.1.call-start = ((), (), s32[]{:S(2)}) async-start(), calls=%async_computation | async-start | bytes 1048576 | tf_op jit(solution)/shard_map/psum | solution.py:273
  124.6 212.1 %copy-start = (f32[2,256,512]{2,1,0:T(8,128)S(1)}, f32[2,256,512]{2,1,0:T(8,128)}, u32[]{:S(2)}) copy-start(f32[2,256,512]{2,1,0:T(8,128)} %get-tuple-element.4) | copy-start | bytes 3145732
  274.0 65.5 %copy-start.1 = (f32[256,256]{0,1:T(8,128)S(1)}, f32[256,256]{0,1:T(8,128)}, u32[]{:S(2)}) copy-start(f32[256,256]{0,1:T(8,128)} %get-tuple-element.23) | copy-start | bytes 786436
Sparse Core Ops, SparseCore 0:
  128.1 145.8 all-reduce.3

commit v2 on v1

--- a/solution.py
+++ b/solution.py
@@ -13,6 +13,10 @@
 F32 = jnp.float32
 BF16 = jnp.bfloat16
 MESH = pl.DeviceIdType.MESH
+HIGHEST = lax.Precision.HIGHEST
+MATES = 2 * PARTS
+PIECE = 2 * M // MATES
+NB = 64
 
 
 def dot_nn(left, right):
@@ -21,6 +25,13 @@
 
 def dot_nt(left, right):
     return lax.dot_general(left, right, (((1,), (1,)), ((), ())), preferred_element_type=F32)
+
+
+def exact_dot(left, right, left_dim, right_dim):
+    return lax.dot_general(
+        left, right, (((left_dim,), (right_dim,)), ((), ())),
+        precision=HIGHEST, preferred_element_type=F32,
+    )
 
 
 def complex_rows(rows, matrix):
@@ -31,10 +42,11 @@
 
 
 def filter_kernel(
-    f_hbm, u_hbm, g_hbm, i_hbm, pole_ref, y_ref, z_ref,
+    f_hbm, u_hbm, g_hbm, i_hbm, pole_ref, y_ref, sum_ref,
     f_raw, f_rows, u_mat, g_mat, i_mat, work, first_s, lifted_d,
     t_send, t_recv, c_send, c_recv, terms, core_recv, far_recv,
-    f_sem, u_sem, g_sem, i_sem, t_ss, t_rs, c_ss, c_rs, q_ss, q_rs, y_ss, y_rs,
+    z_own, parts, core_part, mine, pieces,
+    f_sem, u_sem, g_sem, i_sem, t_ss, t_rs, c_ss, c_rs, q_ss, q_rs, y_ss, y_rs, a_ss, a_rs,
 ):
     pole = lax.axis_index("pole")
     dom = lax.axis_index("dom")
@@ -60,8 +72,19 @@
     interface_load.start()
 
     barrier = pltpu.get_barrier_semaphore()
-    for mate in (core_mate, side_mate, (pole, upper), (pole, lower)):
-        pl.semaphore_signal(barrier, inc=1, device_id=mate, device_id_type=MESH)
+    place = side * PARTS + dom
+
+    def mate_of(step):
+        other = lax.rem(place + step, MATES)
+        return other, (2 * (other // PARTS) + core, lax.rem(other, PARTS))
+
+    pl.semaphore_signal(barrier, inc=1, device_id=core_mate, device_id_type=MESH)
+
+    def greet(step, carry):
+        pl.semaphore_signal(barrier, inc=1, device_id=mate_of(step)[1], device_id_type=MESH)
+        return carry
+
+    lax.fori_loop(1, MATES, greet, 0)
 
     real_z = pole_ref[0, 0]
     imag_z = pole_ref[0, 1]
@@ -193,7 +216,7 @@
                 far_copy(half, quad).start()
 
     first_solve(0)
-    pl.semaphore_wait(barrier, 4)
+    pl.semaphore_wait(barrier, MATES)
     t_copy(0).start()
     interface_load.wait()
     wait_coupling(PB - 1)
@@ -211,7 +234,59 @@
         far_copy(half, 0).wait()
         for i in range(2):
             y_ref[i, half * H : (half + 1) * H, :] = core_recv[half, side, i, 0] + far_recv[half, i, 0]
-            z_ref[i, half * H : (half + 1) * H, :] = core_recv[half, side, i, 1] + far_recv[half, i, 1]
+            z_own[i, half * H : (half + 1) * H, :] = core_recv[half, side, i, 1] + far_recv[half, i, 1]
+
+    gram = exact_dot(y_ref[0], y_ref[0], 1, 1) + exact_dot(y_ref[1], y_ref[1], 1, 1)
+    projected = exact_dot(y_ref[0], z_own[0], 1, 1) + exact_dot(y_ref[1], z_own[1], 1, 1)
+    for i, part in enumerate((gram, projected)):
+        parts[i, :M] = part[:, :H]
+        parts[i, M:] = part[:, H:]
+
+    def waited(ref, sem):
+        pltpu.make_async_copy(ref, ref, sem).wait()
+
+    swap = pltpu.make_async_remote_copy(
+        src_ref=parts.at[1 - core], dst_ref=core_part, send_sem=a_ss.at[0], recv_sem=a_rs.at[0],
+        device_id=core_mate, device_id_type=MESH,
+    )
+    swap.start()
+    swap.wait()
+    mine[...] = parts[core] + core_part[...]
+
+    def scatter(step, carry):
+        other, device = mate_of(step)
+        pltpu.make_async_remote_copy(
+            src_ref=mine.at[pl.ds(pl.multiple_of(other * PIECE, PIECE), PIECE)],
+            dst_ref=pieces.at[step], send_sem=a_ss.at[1], recv_sem=a_rs.at[1],
+            device_id=device, device_id_type=MESH,
+        ).start()
+        return carry
+
+    lax.fori_loop(1, MATES, scatter, 0)
+    own = pl.ds(pl.multiple_of(place * PIECE, PIECE), PIECE)
+    waited(pieces.at[pl.ds(1, MATES - 1)], a_rs.at[1])
+    waited(pieces.at[pl.ds(1, MATES - 1)], a_ss.at[1])
+    pieces[0] = mine[own]
+    sum_ref[core, own] = jnp.sum(pieces[...], axis=0) / (PARTS * PB * B)
+
+    def gather(step, carry):
+        pltpu.make_async_remote_copy(
+            src_ref=sum_ref.at[core, own], dst_ref=sum_ref.at[core, own],
+            send_sem=a_ss.at[2], recv_sem=a_rs.at[2],
+            device_id=mate_of(step)[1], device_id_type=MESH,
+        ).start()
+        return carry
+
+    lax.fori_loop(1, MATES, gather, 0)
+    waited(pieces.at[pl.ds(1, MATES - 1)], a_rs.at[2])
+    waited(pieces.at[pl.ds(1, MATES - 1)], a_ss.at[2])
+    swap = pltpu.make_async_remote_copy(
+        src_ref=sum_ref.at[core], dst_ref=sum_ref.at[core],
+        send_sem=a_ss.at[3], recv_sem=a_rs.at[3],
+        device_id=core_mate, device_id_type=MESH,
+    )
+    swap.start()
+    swap.wait()
 
 
 def filtered_sums(f, u, g, interface, pole_values):
@@ -219,7 +294,7 @@
     dma = pltpu.SemaphoreType.DMA
     return pl.pallas_call(
         filter_kernel,
-        out_shape=(own, own),
+        out_shape=(own, jax.ShapeDtypeStruct((2, 2 * M, H), F32)),
         in_specs=[pl.BlockSpec(memory_space=pl.ANY)] * 4 + [pl.BlockSpec(memory_space=pltpu.SMEM)],
         out_specs=(pl.BlockSpec(memory_space=pltpu.VMEM), pl.BlockSpec(memory_space=pltpu.VMEM)),
         scratch_shapes=[
@@ -238,9 +313,14 @@
             pltpu.VMEM((2, PB, 2, H, B), F32),
             pltpu.VMEM((2, 2, 2, 2, H, B), F32),
             pltpu.VMEM((2, 2, 2, H, B), F32),
+            pltpu.VMEM((2, M, B), F32),
+            pltpu.VMEM((2, 2 * M, H), F32),
+            pltpu.VMEM((2 * M, H), F32),
+            pltpu.VMEM((2 * M, H), F32),
+            pltpu.VMEM((MATES, PIECE, H), F32),
             dma((PB,)), dma((PB,)), dma((PB,)), dma,
             dma((2,)), dma((2,)), dma((2,)), dma((2,)),
-            dma((2, 2)), dma((2, 2)), dma((2,)), dma((2,)),
+            dma((2, 2)), dma((2, 2)), dma((2,)), dma((2,)), dma((4,)), dma((4,)),
         ],
         compiler_params=pltpu.CompilerParams(
             collective_id=0, has_side_effects=True, vmem_limit_bytes=60 * 2**20
@@ -249,42 +329,83 @@
     )(f, u, g, interface, pole_values)
 
 
-def lower_solve(factor, right_side):
-    return lax.linalg.triangular_solve(factor, right_side, left_side=True, lower=True)
-
-
-def row_products(left, right):
-    return jnp.einsum(
-        "bvk,bwk->vw", left, right,
-        precision=lax.Precision.HIGHEST, preferred_element_type=F32,
-    )
+def factor_block(block, work, inverse):
+    wide = (8, 2 * NB)
+    row = lax.broadcasted_iota(jnp.int32, (NB, NB), 0)
+    column = lax.broadcasted_iota(jnp.int32, (NB, NB), 1)
+    work[...] = jnp.concatenate([block, jnp.where(row == column, 1.0, 0.0)], axis=1)
+    place = lax.broadcasted_iota(jnp.int32, wide, 0)
+    for first in range(0, NB, 8):
+        rows = work[first : first + 8, :]
+        spread = [
+            jnp.broadcast_to(rows[:, first + j : first + j + 1], wide) for j in range(8)
+        ]
+        scales = jnp.zeros(wide, F32)
+        for j in range(8):
+            scale = 1.0 / jnp.broadcast_to(spread[j][j : j + 1], wide)
+            scales = jnp.where(place == j, scale, scales)
+            if j < 7:
+                ratio = jnp.where(place > j, spread[j] * scale, 0.0)
+                rows = rows - ratio * jnp.broadcast_to(rows[j : j + 1], wide)
+                for i in range(j + 1, 8):
+                    spread[i] = spread[i] - ratio * jnp.broadcast_to(spread[i][j : j + 1], wide)
+        inverse[first : first + 8, :] = rows * jnp.sqrt(scales)
+        if first + 8 < NB:
+            change = exact_dot(rows * scales, rows, 0, 0)
+            work[first + 8 :, :] = work[first + 8 :, :] - change[first + 8 : NB]
+
+
+def basis_kernel(sum_ref, y_ref, basis_ref, rayleigh_ref, wide, work, block, inverse):
+    row = lax.broadcasted_iota(jnp.int32, (M, M), 0)
+    column = lax.broadcasted_iota(jnp.int32, (M, M), 1)
+    wide[:, :H] = sum_ref[0, :M]
+    wide[:, H:M] = sum_ref[0, M:]
+    wide[:, M:] = jnp.where(row == column, 1.0, 0.0)
+    for low in range(0, M, NB):
+        high = low + NB
+        factor_block(wide[low:high, low:high], work, block)
+        reduced = exact_dot(block[:, NB:], wide[low:high, :], 1, 0)
+        inverse[low:high, :] = reduced[:, M:]
+        if high < M:
+            change = exact_dot(reduced[:, :M], reduced, 0, 0)
+            wide[high:, :] = wide[high:, :] - change[high:]
+    projected = jnp.concatenate([sum_ref[1, :M], sum_ref[1, M:]], axis=1)
+    middle = exact_dot(inverse[...], projected, 1, 0)
+    rayleigh_ref[...] = exact_dot(middle, inverse[...], 1, 1)
+    for i in range(2):
+        basis_ref[i] = exact_dot(inverse[...], y_ref[i], 1, 0).T
+
+
+def orthonormal_basis(sums, y_rows):
+    return pl.pallas_call(
+        basis_kernel,
+        out_shape=(
+            jax.ShapeDtypeStruct((2, B, M), F32),
+            jax.ShapeDtypeStruct((M, M), F32),
+        ),
+        in_specs=[pl.BlockSpec(memory_space=pltpu.VMEM)] * 2,
+        out_specs=(pl.BlockSpec(memory_space=pltpu.VMEM), pl.BlockSpec(memory_space=pltpu.VMEM)),
+        scratch_shapes=[
+            pltpu.VMEM((M, 2 * M), F32),
+            pltpu.VMEM((NB, 2 * NB), F32),
+            pltpu.VMEM((NB, 2 * NB), F32),
+            pltpu.VMEM((M, M), F32),
+        ],
+        compiler_params=pltpu.CompilerParams(vmem_limit_bytes=32 * 2**20),
+        name="orthonormal_basis",
+    )(sums, y_rows)
 
 
 def on_device(initial_block, coupling, pivots, interface, pole_values):
-    y_rows, z_rows = filtered_sums(
+    y_rows, sums = filtered_sums(
         initial_block[0],
         coupling[0],
         pivots[0, 0].reshape(PB, 2 * B, B),
         interface[0, 0].reshape(3, 2 * B, B),
         pole_values,
     )
-    gram_part = row_products(y_rows, y_rows)
-    projected_part = row_products(y_rows, z_rows)
-    gram_total, projected_total = lax.psum((gram_part, projected_part), ("pole", "dom"))
-    row_total = PB * B * PARTS
-    gram = gram_total / row_total
-    projected = projected_total / row_total
-    factor = jnp.linalg.cholesky(gram)
-    inverse = lower_solve(factor, jnp.eye(M, dtype=F32))
-    filtered_basis = jnp.einsum(
-        "bvk,wv->bkw", y_rows, inverse,
-        precision=lax.Precision.HIGHEST, preferred_element_type=F32,
-    )[None]
-    middle = jnp.dot(inverse, projected, precision=lax.Precision.HIGHEST)
-    rayleigh = lax.dot_general(
-        middle, inverse, (((1,), (1,)), ((), ())), precision=lax.Precision.HIGHEST
-    )
-    return (filtered_basis, rayleigh)
+    basis, rayleigh = orthonormal_basis(sums, y_rows)
+    return (basis[None], rayleigh)
 
 
 def solution(mesh):

time: 348 us -> 160 us (0.46)
  waiting for transfers between devices: 146 us -> 0 us
  other arithmetic: 55.9 us -> 0 us
  Pallas kernels: 114 us -> 157 us
  between operations: 15.5 us -> 0.65 us
  matrix products: 12.3 us -> 0 us
    psum x1 -> x0, waiting for transfers between devices: 146 us -> none  [on_device(): lax.psum((gram_part, projected_part), ('pole', 'dom'))]
    another operation x9 -> x0, other arithmetic: 53.8 us -> none  [the longest x6 34.1 us: on_device(): factor = jnp.linalg.cholesky(gram)]
    pallas_call x1 -> x2, Pallas kernels: 114 us -> 157 us  [the longest x1 137 us: filtered_sums(): pl.pallas_call(filter_kernel, out_shape=(own, jax.ShapeDtypeStruct((2, 2...]
    dot_general x5 -> x0, matrix products: 10.9 us -> none  [the longest x2 6.64 us: row_products(): jnp.einsum('bvk,bwk->vw', left, right, precision=lax.Precision.HIGHEST, p...]
    another operation x9 -> x0, local copies, waits for them, and re-layouts: 4.05 us -> none
  transfers between devices with their start and end apart: 1 -> 0, of which waited for: 1 -> 0; matrix products, arithmetic and copies ran while one was open for 0% -> 0% of each run, Pallas kernels for 0% -> 0%
where the time goes in v2:
time: 160 us
  Pallas kernels  157 us (98%)
  local copies, waits for them, and re-layouts  2.26 us (1%)
    pallas_call x1, Pallas kernels, filtered_sums(): pl.pallas_call(filter_kernel, out_shape=(own, jax.ShapeDtypeStruct((2, 2...  137 us
    pallas_call x1, Pallas kernels, orthonormal_basis(): pl.pallas_call(basis_kernel, out_shape=(jax.ShapeDtypeStruct((2, B, M), F...  19.9 us

profile of v2, /device:TPU:1, one launch (start us, length us, event | category | flops | bytes accessed | tf_op | source)
XLA Modules:
  0.0 159.5 jit_solution(7943358960237802681)
XLA Ops:
  0.6 136.7 %filter_sums.1 = (f32[2,256,512]{2,1,0:T(8,128)}, f32[2,512,128]{2,1,0:T(8,128)}) custom-call(bf16[8,512,256]{2,1,0:T(8,128)(2,1)} %bitcast.8, bf16[8,512,512]{2,1,0:T(8,128)(2,1)} %bitcast.6, bf16[8,1024,512]{2,1,0:T(8,128)(2,1)} %bitcast.5, bf16[3,1024,512]{2,1,0:T(8,128)(2,1)} %bitcast.7, f32[1,4]{1,0:T(1,128)} %pole_ref.1), custom_call_target="tpu_custom_call" | custom-call | tf_op jit(solution)/shard_map/filter_sums/pallas_call | solution.py:295
  137.4 0.0 copy-start
  137.4 1.2 copy-done
  138.6 0.0 copy-start.1
  138.6 1.0 copy-done.1
  139.6 19.9 %orthonormal_basis.1 = (f32[2,512,256]{2,1,0:T(8,128)}, f32[256,256]{1,0:T(8,128)}) custom-call(f32[2,512,128]{2,1,0:T(8,128)S(1)} %copy-done.1, f32[2,256,512]{2,1,0:T(8,128)S(1)} %copy-done), custom_call_target="tpu_custom_call" | custom-call | tf_op jit(solution)/shard_map/orthonormal_basis/pallas_call | solution.py:380
Async XLA Ops:
  137.4 1.2 copy-start
  138.6 1.0 copy-start.1

commit v3 on v2

--- a/solution.py
+++ b/solution.py
@@ -17,6 +17,7 @@
 MATES = 2 * PARTS
 PIECE = 2 * M // MATES
 NB = 64
+SPAN = 16
 
 
 def dot_nn(left, right):
@@ -329,33 +330,40 @@
     )(f, u, g, interface, pole_values)
 
 
-def factor_block(block, work, inverse):
-    wide = (8, 2 * NB)
+def factor_block(block, inverse):
+    shape = (8, 2 * NB)
+    groups = NB // 8
     row = lax.broadcasted_iota(jnp.int32, (NB, NB), 0)
     column = lax.broadcasted_iota(jnp.int32, (NB, NB), 1)
-    work[...] = jnp.concatenate([block, jnp.where(row == column, 1.0, 0.0)], axis=1)
-    place = lax.broadcasted_iota(jnp.int32, wide, 0)
-    for first in range(0, NB, 8):
-        rows = work[first : first + 8, :]
-        spread = [
-            jnp.broadcast_to(rows[:, first + j : first + j + 1], wide) for j in range(8)
-        ]
-        scales = jnp.zeros(wide, F32)
-        for j in range(8):
-            scale = 1.0 / jnp.broadcast_to(spread[j][j : j + 1], wide)
-            scales = jnp.where(place == j, scale, scales)
-            if j < 7:
-                ratio = jnp.where(place > j, spread[j] * scale, 0.0)
-                rows = rows - ratio * jnp.broadcast_to(rows[j : j + 1], wide)
-                for i in range(j + 1, 8):
-                    spread[i] = spread[i] - ratio * jnp.broadcast_to(spread[i][j : j + 1], wide)
-        inverse[first : first + 8, :] = rows * jnp.sqrt(scales)
-        if first + 8 < NB:
-            change = exact_dot(rows * scales, rows, 0, 0)
-            work[first + 8 :, :] = work[first + 8 :, :] - change[first + 8 : NB]
-
-
-def basis_kernel(sum_ref, y_ref, basis_ref, rayleigh_ref, wide, work, block, inverse):
+    start = jnp.concatenate([block, jnp.where(row == column, 1.0, 0.0)], axis=1)
+    place = lax.broadcasted_iota(jnp.int32, shape, 0)
+    rows = [start[8 * g : 8 * g + 8, :] for g in range(groups)]
+    scales = [jnp.zeros(shape, F32) for g in range(groups)]
+    for first in range(0, NB, SPAN):
+        spread = {
+            (g, j): jnp.broadcast_to(rows[g][:, first + j : first + j + 1], shape)
+            for g in range(first // 8, groups)
+            for j in range(SPAN)
+        }
+        for j in range(SPAN):
+            pivot, at = divmod(first + j, 8)
+            scale = 1.0 / jnp.broadcast_to(spread[pivot, j][at : at + 1], shape)
+            scales[pivot] = jnp.where(place == at, scale, scales[pivot])
+            pivot_row = jnp.broadcast_to(rows[pivot][at : at + 1], shape) * scale
+            rest = range(j + 1, SPAN)
+            across = [jnp.broadcast_to(spread[pivot, i][at : at + 1], shape) * scale for i in rest]
+            for g in range(pivot, groups):
+                taken = spread[g, j]
+                if g == pivot:
+                    taken = jnp.where(place > at, taken, 0.0)
+                rows[g] = rows[g] - taken * pivot_row
+                for i, value in zip(rest, across):
+                    spread[g, i] = spread[g, i] - taken * value
+    for g in range(groups):
+        inverse[8 * g : 8 * g + 8, :] = rows[g] * jnp.sqrt(scales[g])
+
+
+def basis_kernel(sum_ref, y_ref, basis_ref, rayleigh_ref, wide, block, inverse):
     row = lax.broadcasted_iota(jnp.int32, (M, M), 0)
     column = lax.broadcasted_iota(jnp.int32, (M, M), 1)
     wide[:, :H] = sum_ref[0, :M]
@@ -363,7 +371,7 @@
     wide[:, M:] = jnp.where(row == column, 1.0, 0.0)
     for low in range(0, M, NB):
         high = low + NB
-        factor_block(wide[low:high, low:high], work, block)
+        factor_block(wide[low:high, low:high], block)
         reduced = exact_dot(block[:, NB:], wide[low:high, :], 1, 0)
         inverse[low:high, :] = reduced[:, M:]
         if high < M:
@@ -388,7 +396,6 @@
         scratch_shapes=[
             pltpu.VMEM((M, 2 * M), F32),
             pltpu.VMEM((NB, 2 * NB), F32),
-            pltpu.VMEM((NB, 2 * NB), F32),
             pltpu.VMEM((M, M), F32),
         ],
         compiler_params=pltpu.CompilerParams(vmem_limit_bytes=32 * 2**20),

time: 160 us -> 152 us (0.950)
  Pallas kernels: 157 us -> 149 us
    pallas_call x1, Pallas kernels: 19.9 us -> 12.2 us  [orthonormal_basis(): pl.pallas_call(basis_kernel, out_shape=(jax.ShapeDtypeStruct((2, B, M), F...]
where the time goes in v3:
time: 152 us
  Pallas kernels  149 us (98%)
  local copies, waits for them, and re-layouts  2.26 us (1%)
    pallas_call x1, Pallas kernels, filtered_sums(): pl.pallas_call(filter_kernel, out_shape=(own, jax.ShapeDtypeStruct((2, 2...  137 us
    pallas_call x1, Pallas kernels, orthonormal_basis(): pl.pallas_call(basis_kernel, out_shape=(jax.ShapeDtypeStruct((2, B, M), F...  12.2 us

profile of v3, /device:TPU:1, one launch (start us, length us, event | category | flops | bytes accessed | tf_op | source)
XLA Modules:
  0.0 151.8 jit_solution(17567914594667692505)
XLA Ops:
  0.6 136.7 %filter_sums.1 = (f32[2,256,512]{2,1,0:T(8,128)}, f32[2,512,128]{2,1,0:T(8,128)}) custom-call(bf16[8,512,256]{2,1,0:T(8,128)(2,1)} %bitcast.8, bf16[8,512,512]{2,1,0:T(8,128)(2,1)} %bitcast.6, bf16[8,1024,512]{2,1,0:T(8,128)(2,1)} %bitcast.5, bf16[3,1024,512]{2,1,0:T(8,128)(2,1)} %bitcast.7, f32[1,4]{1,0:T(1,128)} %pole_ref.1), custom_call_target="tpu_custom_call" | custom-call | tf_op jit(solution)/shard_map/filter_sums/pallas_call | solution.py:296
  137.4 0.0 copy-start
  137.4 1.2 copy-done
  138.6 0.0 copy-start.1
  138.6 1.0 copy-done.1
  139.6 12.2 %orthonormal_basis.1 = (f32[2,512,256]{2,1,0:T(8,128)}, f32[256,256]{1,0:T(8,128)}) custom-call(f32[2,512,128]{2,1,0:T(8,128)S(1)} %copy-done.1, f32[2,256,512]{2,1,0:T(8,128)S(1)} %copy-done), custom_call_target="tpu_custom_call" | custom-call | tf_op jit(solution)/shard_map/orthonormal_basis/pallas_call | solution.py:388
Async XLA Ops:
  137.4 1.2 copy-start
  138.6 1.0 copy-start.1

commit v4 on v3

--- a/solution.py
+++ b/solution.py
@@ -149,19 +149,26 @@
             device_id=(pole, lower), device_id_type=MESH,
         )
 
-    def core_copy(half, quad):
-        start = 4 * quad + 2 * (1 - core)
+    def core_copy(half, quad, i):
         return pltpu.make_async_remote_copy(
-            src_ref=terms.at[half, pl.ds(start, 2)], dst_ref=core_recv.at[half, quad],
-            send_sem=q_ss.at[half, quad], recv_sem=q_rs.at[half, quad],
+            src_ref=terms.at[half, 4 * quad + 2 * (1 - core) + i],
+            dst_ref=core_recv.at[half, quad, i],
+            send_sem=q_ss.at[half, quad, i], recv_sem=q_rs.at[half, quad, i],
             device_id=core_mate, device_id_type=MESH,
         )
 
-    def far_copy(half, quad):
+    def far_copy(half, i, kind):
         return pltpu.make_async_remote_copy(
-            src_ref=core_recv.at[half, quad], dst_ref=far_recv.at[half],
-            send_sem=y_ss.at[half], recv_sem=y_rs.at[half],
+            src_ref=core_recv.at[half, 1 - side, i, kind], dst_ref=far_recv.at[half, i, kind],
+            send_sem=y_ss.at[half, i, kind], recv_sem=y_rs.at[half, i, kind],
             device_id=side_mate, device_id_type=MESH,
+        )
+
+    def far_sum(half, i, kind):
+        far_copy(half, i, kind).wait()
+        target = (y_ref, z_own)[kind]
+        target[i, half * H : (half + 1) * H, :] = (
+            core_recv[half, side, i, kind] + far_recv[half, i, kind]
         )
 
     def interface(half):
@@ -203,18 +210,21 @@
             return carry
 
         lax.fori_loop(0, 3, backward, 0)
-        core_copy(half, 1).start()
+        for i in (1, 0):
+            core_copy(half, 1, i).start()
         lax.fori_loop(3, PB - 1, backward, 0)
-        core_copy(half, 0).start()
+        for i in (1, 0):
+            core_copy(half, 0, i).start()
 
         for quad in (1, 0):
-            core_copy(half, quad).wait()
-            for i in range(2):
+            for i in (1, 0):
+                core_copy(half, quad, i).wait()
                 core_recv[half, quad, i] += terms[half, 4 * quad + 2 * core + i]
 
-            @pl.when(side == 1 - quad)
-            def _():
-                far_copy(half, quad).start()
+                @pl.when(side == 1 - quad)
+                def _():
+                    for kind in range(2):
+                        far_copy(half, i, kind).start()
 
     first_solve(0)
     pl.semaphore_wait(barrier, MATES)
@@ -231,17 +241,19 @@
     for half in range(2):
         c_copy(half).wait()
         second_solve(half)
-    for half in range(2):
-        far_copy(half, 0).wait()
-        for i in range(2):
-            y_ref[i, half * H : (half + 1) * H, :] = core_recv[half, side, i, 0] + far_recv[half, i, 0]
-            z_own[i, half * H : (half + 1) * H, :] = core_recv[half, side, i, 1] + far_recv[half, i, 1]
-
-    gram = exact_dot(y_ref[0], y_ref[0], 1, 1) + exact_dot(y_ref[1], y_ref[1], 1, 1)
-    projected = exact_dot(y_ref[0], z_own[0], 1, 1) + exact_dot(y_ref[1], z_own[1], 1, 1)
-    for i, part in enumerate((gram, projected)):
-        parts[i, :M] = part[:, :H]
-        parts[i, M:] = part[:, H:]
+    for i in (1, 0):
+        for kind in range(2):
+            far_sum(0, i, kind)
+    for i in (1, 0):
+        for kind in range(2):
+            far_sum(1, i, kind)
+            product = exact_dot(y_ref[i], (y_ref, z_own)[kind][i], 1, 1)
+            if i == 1:
+                parts[kind, :M] = product[:, :H]
+                parts[kind, M:] = product[:, H:]
+            else:
+                parts[kind, :M] += product[:, :H]
+                parts[kind, M:] += product[:, H:]
 
     def waited(ref, sem):
         pltpu.make_async_copy(ref, ref, sem).wait()
@@ -321,7 +333,7 @@
             pltpu.VMEM((MATES, PIECE, H), F32),
             dma((PB,)), dma((PB,)), dma((PB,)), dma,
             dma((2,)), dma((2,)), dma((2,)), dma((2,)),
-            dma((2, 2)), dma((2, 2)), dma((2,)), dma((2,)), dma((4,)), dma((4,)),
+            dma((2, 2, 2)), dma((2, 2, 2)), dma((2, 2, 2)), dma((2, 2, 2)), dma((4,)), dma((4,)),
         ],
         compiler_params=pltpu.CompilerParams(
             collective_id=0, has_side_effects=True, vmem_limit_bytes=60 * 2**20
@@ -363,7 +375,9 @@
         inverse[8 * g : 8 * g + 8, :] = rows[g] * jnp.sqrt(scales[g])
 
 
-def basis_kernel(sum_ref, y_ref, basis_ref, rayleigh_ref, wide, block, inverse):
+def basis_kernel(sum_ref, y_hbm, basis_ref, rayleigh_ref, wide, block, inverse, y_ref, y_sem):
+    load = pltpu.make_async_copy(y_hbm, y_ref, y_sem)
+    load.start()
     row = lax.broadcasted_iota(jnp.int32, (M, M), 0)
     column = lax.broadcasted_iota(jnp.int32, (M, M), 1)
     wide[:, :H] = sum_ref[0, :M]
@@ -380,6 +394,7 @@
     projected = jnp.concatenate([sum_ref[1, :M], sum_ref[1, M:]], axis=1)
     middle = exact_dot(inverse[...], projected, 1, 0)
     rayleigh_ref[...] = exact_dot(middle, inverse[...], 1, 1)
+    load.wait()
     for i in range(2):
         basis_ref[i] = exact_dot(inverse[...], y_ref[i], 1, 0).T
 
@@ -391,14 +406,16 @@
             jax.ShapeDtypeStruct((2, B, M), F32),
             jax.ShapeDtypeStruct((M, M), F32),
         ),
-        in_specs=[pl.BlockSpec(memory_space=pltpu.VMEM)] * 2,
+        in_specs=[pl.BlockSpec(memory_space=pltpu.VMEM), pl.BlockSpec(memory_space=pl.ANY)],
         out_specs=(pl.BlockSpec(memory_space=pltpu.VMEM), pl.BlockSpec(memory_space=pltpu.VMEM)),
         scratch_shapes=[
             pltpu.VMEM((M, 2 * M), F32),
             pltpu.VMEM((NB, 2 * NB), F32),
             pltpu.VMEM((M, M), F32),
+            pltpu.VMEM((2, M, B), F32),
+            pltpu.SemaphoreType.DMA,
         ],
-        compiler_params=pltpu.CompilerParams(vmem_limit_bytes=32 * 2**20),
+        compiler_params=pltpu.CompilerParams(vmem_limit_bytes=60 * 2**20),
         name="orthonormal_basis",
     )(sums, y_rows)
 

time: 152 us -> 150 us (0.987)
  local copies, waits for them, and re-layouts: 2.26 us -> 0 us
    unnamed x4 -> x0, local copies, waits for them, and re-layouts: 2.26 us -> none
where the time goes in v4:
time: 150 us
  Pallas kernels  149 us (99%)
    pallas_call x1, Pallas kernels, filtered_sums(): pl.pallas_call(filter_kernel, out_shape=(own, jax.ShapeDtypeStruct((2, 2...  135 us
    pallas_call x1, Pallas kernels, orthonormal_basis(): pl.pallas_call(basis_kernel, out_shape=(jax.ShapeDtypeStruct((2, B, M), F...  13.5 us

profile of v4, /device:TPU:1, one launch (start us, length us, event | category | flops | bytes accessed | tf_op | source)
XLA Modules:
  0.0 149.6 jit_solution(11061950180105979125)
XLA Ops:
  0.6 135.3 %filter_sums.1 = (f32[2,256,512]{2,1,0:T(8,128)}, f32[2,512,128]{2,1,0:T(8,128)}) custom-call(bf16[8,512,256]{2,1,0:T(8,128)(2,1)} %bitcast.8, bf16[8,512,512]{2,1,0:T(8,128)(2,1)} %bitcast.6, bf16[8,1024,512]{2,1,0:T(8,128)(2,1)} %bitcast.5, bf16[3,1024,512]{2,1,0:T(8,128)(2,1)} %bitcast.7, f32[1,4]{1,0:T(1,128)} %pole_ref.1), custom_call_target="tpu_custom_call" | custom-call | tf_op jit(solution)/shard_map/filter_sums/pallas_call | solution.py:308
  135.9 13.5 %orthonormal_basis.1 = (f32[2,512,256]{2,1,0:T(8,128)}, f32[256,256]{1,0:T(8,128)}) custom-call(f32[2,512,128]{2,1,0:T(8,128)} %get-tuple-element.6.sum_ref, f32[2,256,512]{2,1,0:T(8,128)} %get-tuple-element.7.y_hbm), custom_call_target="tpu_custom_call" | custom-call | tf_op jit(solution)/shard_map/orthonormal_basis/pallas_call | solution.py:403
